TPU v7x, 128 devices: a whole 4x4x4 slice. The times are simulated.
128 devices in a mesh: lon: 16 (over x_hi, z, core), lat: 8 (over y, x_lo).
Axes of the slice: x: 4 (x_hi: 2, x_lo: 2; x = x_hi * 2 + x_lo), y: 4, z: 4, core: 2. Of those that a mesh axis runs over, the one named last changes fastest.
Arguments:
- heat_anomaly_values: float32 [10, 512, 4096], P(None, 'lat', 'lon'), may hold values from -6 to 6
- saltiness_anomaly: float32 [10, 512, 4096], P(None, 'lat', 'lon'), may hold values from -6 to 6
- zonal_speed: float32 [10, 512, 4096], P(None, 'lat', 'lon'), may hold values from -3 to 3
- meridional_speed: float32 [10, 512, 4096], P(None, 'lat', 'lon'), may hold values from -3 to 3
- marine_site_indicator: int32 [10, 512, 4096], P(None, 'lat', 'lon'), may hold values 0 or 1
- layer_boundary_mixing_rate: float32 [9, 512, 4096], P(None, 'lat', 'lon'), may hold values from 0.05 to 5
- layer_spacing: float32 [10], replicated, may hold values from 0.5 to 2
- planetary_spin_rate: float32 [512], P('lat'), may hold values from 0.4 to 2
- seam_hinge_variety: int32 [1], replicated, may hold values from 0 to 1
- seam_partner_meridian: int32 [4096], P('lon'), may hold values from 0 to 4095, as said below
Outputs:
- temperature_next: float32 [10, 512, 4096], P(None, 'lat', 'lon')
- salinity_next: float32 [10, 512, 4096], P(None, 'lat', 'lon')
- eastward_next: float32 [10, 512, 4096], P(None, 'lat', 'lon')
- northward_next: float32 [10, 512, 4096], P(None, 'lat', 'lon')
Inputs may be any that keep to these rules, and one draw needn't show every extreme that they name: seam_partner_meridian[i] = (c * 256 - 1 - i) mod 4096 for one whole number c drawn for the run: each longitude is paired with its mirror about a tile boundary.
All inputs are finite; a program needn't handle non-finite values. No bound on the sum of `marine_site_indicator` on one device may be relied on, other than what follows from the above.
Results may differ from a plain program's by a relative error of at most 0.00002.
Values sent between devices are 32-bit elements; how exact they have to be, the bound alone decides.
No kernel may reach another device: no remote copies, remote signals or barrier semaphores. Data moves between devices by JAX's collectives and lax.ppermute only.
A program may use at most 128 MiB of HBM per device.

v0:
```python
import jax
import jax.numpy as jnp
from jax import lax
from jax.sharding import PartitionSpec as P

time_step = 0.2
tracer_mixing = 0.3
momentum_mixing = 0.3
thermal_coeff = 0.2
haline_coeff = 0.8
gravity = 0.1


def padded_2(cells, sides, width):
    for axis, dim in sides:
        count = lax.axis_size(axis)
        head = lax.slice_in_dim(cells, 0, width, axis=dim)
        tail = lax.slice_in_dim(cells, cells.shape[dim] - width, cells.shape[dim], axis=dim)
        cells = jnp.concatenate(
            [
                lax.ppermute(tail, axis, [(i, (i + 1) % count) for i in range(count)]),
                cells,
                lax.ppermute(head, axis, [((i + 1) % count, i) for i in range(count)]),
            ],
            axis=dim,
        )
    return cells


def fold_source(piled_quantities, seam_hinge_variety):
    row_count = piled_quantities.shape[2]
    return lax.dynamic_index_in_dim(
        piled_quantities, row_count - 1 - seam_hinge_variety[0], 2, keepdims=False
    )


def close_rim(padded, ghost_row):
    lat_index = lax.axis_index("lat")
    bottom = lat_index == 0
    at_top = lat_index == lax.axis_size("lat") - 1
    padded_rows = padded.shape[2]
    row_place = lax.broadcasted_iota(jnp.int32, (padded_rows, 1), 0)
    south_mask = jnp.logical_and(row_place == 0, bottom)
    north_mask = jnp.logical_and(row_place == padded_rows - 1, at_top)
    ghost_full = jnp.pad(ghost_row, ((0, 0), (0, 0), (1, 1)))[:, :, None, :]
    cleared = jnp.where(south_mask, jnp.float32(0.0), padded)
    return jnp.where(north_mask, ghost_full, cleared)


def neighbours(padded):
    return (
        padded[..., 1:-1, 1:-1],
        padded[..., 1:-1, 2:],
        padded[..., 1:-1, :-2],
        padded[..., 2:, 1:-1],
        padded[..., :-2, 1:-1],
    )


def wet_faces(padded_wet):
    wet_here, wet_e, wet_w, wet_n, wet_s = neighbours(padded_wet)
    return (wet_here, wet_here * wet_e, wet_here * wet_w, wet_here * wet_n, wet_here * wet_s)


def tendency(scalars_plus_ghost_rim, padded_east, padded_north, face_wet):
    wet_here, wet_east, wet_west, wet_north, wet_south = face_wet
    center, value_east, value_west, value_north, value_south = neighbours(scalars_plus_ghost_rim)
    flow_here, flow_east, flow_west, unused_north, unused_south = neighbours(padded_east)
    turn_here, unused_east, unused_west, turn_north, turn_south = neighbours(padded_north)
    face_east = 0.5 * (flow_here + flow_east)
    face_west = 0.5 * (flow_west + flow_here)
    face_north = 0.5 * (turn_here + turn_north)
    face_south = 0.5 * (turn_south + turn_here)
    flux_east = wet_east * (
        jnp.maximum(face_east, 0.0) * center
        + jnp.minimum(face_east, 0.0) * value_east
        - tracer_mixing * (value_east - center)
    )
    flux_west = wet_west * (
        jnp.maximum(face_west, 0.0) * value_west
        + jnp.minimum(face_west, 0.0) * center
        - tracer_mixing * (center - value_west)
    )
    flux_north = wet_north * (
        jnp.maximum(face_north, 0.0) * center
        + jnp.minimum(face_north, 0.0) * value_north
        - tracer_mixing * (value_north - center)
    )
    flux_south = wet_south * (
        jnp.maximum(face_south, 0.0) * value_south
        + jnp.minimum(face_south, 0.0) * center
        - tracer_mixing * (center - value_south)
    )
    return center - time_step * wet_here * (flux_east - flux_west + flux_north - flux_south)


def laplace(padded, face_wet):
    wet_here, wet_east, wet_west, wet_north, wet_south = face_wet
    center, value_east, value_west, value_north, value_south = neighbours(padded)
    return (
        wet_east * (value_east - center)
        + wet_west * (value_west - center)
        + wet_north * (value_north - center)
        + wet_south * (value_south - center)
    )


def hydrostatic(padded_density, layer_spacing):
    layer_weight = padded_density * layer_spacing[:, None, None]
    above = jnp.cumsum(layer_weight, axis=0) - layer_weight
    return gravity * (above + 0.5 * layer_weight)


def momentum(padded_east, padded_north, pressure, coriolis_rows, face_wet):
    wet_here, wet_east, wet_west, wet_north, wet_south = face_wet
    press_here, press_east, press_west, press_north, press_south = neighbours(pressure)
    grad_east = 0.5 * (wet_east * (press_east - press_here) + wet_west * (press_here - press_west))
    grad_north = 0.5 * (
        wet_north * (press_north - press_here) + wet_south * (press_here - press_south)
    )
    flow_here = padded_east[:, 1:-1, 1:-1]
    turn_here = padded_north[:, 1:-1, 1:-1]
    new_east = flow_here + time_step * wet_here * (
        coriolis_rows * turn_here - grad_east + momentum_mixing * laplace(padded_east, face_wet)
    )
    new_north = turn_here + time_step * wet_here * (
        -coriolis_rows * flow_here - grad_north + momentum_mixing * laplace(padded_north, face_wet)
    )
    return jnp.stack([new_east, new_north])


def factor(marine_sites, layer_boundary_mixing_rate, layer_spacing):
    kappa = layer_boundary_mixing_rate * marine_sites[:-1] * marine_sites[1:]
    level_count = marine_sites.shape[0]
    bands = []
    previous = None
    for layer in range(level_count):
        height = layer_spacing[layer]
        if layer > 0:
            lower_band = -time_step * kappa[layer - 1] / height
        else:
            lower_band = jnp.zeros_like(marine_sites[0])
        if layer < level_count - 1:
            upper_band = -time_step * kappa[layer] / height
        else:
            upper_band = jnp.zeros_like(marine_sites[0])
        divisor = 1.0 - lower_band - upper_band
        if previous is not None:
            divisor = divisor - lower_band * previous
        ratio_band = upper_band / divisor
        bands.append((lower_band, divisor, ratio_band))
        previous = ratio_band
    return bands


def solve_columns(bands, right_side):
    level_count = len(bands)
    forward = []
    previous = None
    for layer in range(level_count):
        lower_band, divisor, ratio_band = bands[layer]
        current = right_side[:, layer]
        if previous is not None:
            current = current - lower_band * previous
        previous = current / divisor
        forward.append(previous)
    result = [None] * level_count
    after = forward[-1]
    result[-1] = after
    for layer in reversed(range(level_count - 1)):
        after = forward[layer] - bands[layer][2] * after
        result[layer] = after
    return jnp.stack(result, axis=1)


def on_device(
    heat_anomaly_values,
    saltiness_anomaly,
    zonal_speed,
    meridional_speed,
    marine_site_indicator,
    layer_boundary_mixing_rate,
    layer_spacing,
    planetary_spin_rate,
    seam_hinge_variety,
    seam_partner_meridian,
):
    marine_sites = marine_site_indicator.astype(jnp.float32)
    piled_quantities = jnp.stack(
        [heat_anomaly_values, saltiness_anomaly, zonal_speed, meridional_speed, marine_sites]
    )
    padded = padded_2(piled_quantities, (("lon", 3), ("lat", 2)), 1)
    fold_rows = fold_source(piled_quantities, seam_hinge_variety)
    gathered = lax.all_gather(fold_rows, "lon", axis=2, tiled=True)
    ghost_row = jnp.take(gathered, seam_partner_meridian, axis=2)
    signs = jnp.array([1.0, 1.0, -1.0, -1.0, 1.0], jnp.float32)[:, None, None]
    padded = close_rim(padded, ghost_row * signs)
    padded_east = padded[2]
    padded_north = padded[3]
    face_wet = wet_faces(padded[4])
    tracer_step = tendency(padded[0:2], padded_east, padded_north, face_wet)
    bands = factor(marine_sites, layer_boundary_mixing_rate, layer_spacing)
    new_tracers = solve_columns(bands, tracer_step)
    density = (-thermal_coeff * new_tracers[0] + haline_coeff * new_tracers[1])[None]
    padded_density = padded_2(density, (("lon", 3), ("lat", 2)), 1)
    density_rows = fold_source(density, seam_hinge_variety)
    gathered_density = lax.all_gather(density_rows, "lon", axis=2, tiled=True)
    padded_density = close_rim(
        padded_density, jnp.take(gathered_density, seam_partner_meridian, axis=2)
    )[0]
    pressure = hydrostatic(padded_density, layer_spacing)
    flow_step = momentum(
        padded_east, padded_north, pressure, planetary_spin_rate[None, :, None], face_wet
    )
    new_flows = solve_columns(bands, flow_step)
    return (new_tracers[0], new_tracers[1], new_flows[0], new_flows[1])


def solution(mesh):
    placed = (
        P(None, "lat", "lon"),
        P(None, "lat", "lon"),
        P(None, "lat", "lon"),
        P(None, "lat", "lon"),
        P(None, "lat", "lon"),
        P(None, "lat", "lon"),
        P(),
        P("lat"),
        P(),
        P("lon"),
    )
    return jax.shard_map(
        on_device,
        mesh=mesh,
        in_specs=placed,
        out_specs=(
            P(None, "lat", "lon"),
            P(None, "lat", "lon"),
            P(None, "lat", "lon"),
            P(None, "lat", "lon"),
        ),
        check_vma=False,
    )
```

profile of v0, /device:TPU:26, one launch (start us, length us, event | category | flops | bytes accessed | tf_op | source)
XLA Modules:
  0.0 203.3 jit_solution(4766815486366170467)
XLA Ops:
  3.3 2.3 %fusion.121 = (f32[5,10,64,1]{3,2,1,0:T(8,128)}, f32[5,10,64,1]{3,2,1,0:T(8,128)}) fusion(f32[5,10,64,256]{3,2,1,0:T(8,128)S(1)} %bitcast_dynamic-update-slice_fusion), kind=kLoop, calls=%fused_computation.262 | loop fusion | bytes 51200 | tf_op jit(solution)/shard_map/slice | solution.py:18
  7.6 2.6 %copy.107 = f32[5,10,64,1]{2,3,1,0:T(1,128)} copy(f32[5,10,64,1]{3,2,1,0:T(8,128)} %get-tuple-element.67) | data formatting | bytes 25600
  10.2 5.3 %collective-permute-start.1 = (f32[5,10,64,1]{2,3,1,0:T(1,128)}, f32[5,10,64,1]{2,3,1,0:T(1,128)}, u32[]{:S(2)}, u32[]{:S(2)}) collective-permute-start(f32[5,10,64,1]{2,3,1,0:T(1,128)} %copy.107), channel_id=1, source_target_pairs={{8,0},{16,8},{24,16},{32,24},{40,32},{48,40},{56,48},{64,56},{72,6... | collective-permute-start | bytes 38408 | tf_op jit(solution)/shard_map/ppermute | solution.py:23
  18.2 24.6 %all-gather = f32[5,10,1,4096]{3,2,1,0:T(1,128)} all-gather(f32[5,10,1,256]{3,2,1,0:T(1,128)S(1)} %constant_dynamic-slice_fusion), channel_id=2, replica_groups=mesh['lon'=16,'lat'=8] {'lon'}, dimensions={3}, use_global_device_ids=true | all-gather | bytes 870400 | tf_op jit(solution)/shard_map/all_gather | solution.py:194
  42.8 9.9 %copy.92 = f32[5,10,1,4096]{1,0,3,2:T(8,128)} copy(f32[5,10,1,4096]{3,2,1,0:T(1,128)} %all-gather) | data formatting | bytes 1638400 | tf_op jit(solution)/shard_map/all_gather | solution.py:194
  53.4 7.5 %gather_fusion = f32[256,5,10]{2,1,0:T(8,128)} fusion(f32[5,10,4096]{1,0,2:T(8,128)} %bitcast.106, s32[1024]{0:T(1024)S(1)} %pad_clamp_fusion), kind=kCustom, calls=%fused_computation | custom fusion | bytes 103424 | tf_op jit(solution)/shard_map/jit(_take)/gather | solution.py:195
  62.5 2.6 %fusion.100 = (f32[64,256]{1,0:T(8,128)}, f32[1,64,256]{2,1,0:T(8,128)S(1)}, f32[1,64,256]{2,1,0:T(8,128)S(1)}) fusion(f32[]{:T(128)} %bitcast.19, f32[9,64,256]{2,1,0:T(8,128)S(1)} %slice_multiply_fusion.4, f32[]{:T(128)} %bitcast.15, f32[]{:T(128)} %bitcast.12), kind=kLoop, calls=%fused_computation.251 | loop fusion | flops 376832 | bytes 393228 | tf_op jit(solution)/shard_map/mul | solution.py:171
  65.0 3.9 %fusion.102 = (f32[64,256]{1,0:T(8,128)S(1)}, f32[1,64,256]{2,1,0:T(8,128)S(1)}, f32[1,64,256]{2,1,0:T(8,128)S(1)}, f32[64,256]{1,0:T(8,128)}, f32[64,256]{1,0:T(8,128)}) fusion(f32[]{:T(128)} %bitcast.27, f32[9,64,256]{2,1,0:T(8,128)S(1)} %slice_multiply_fusion.4, f32[]{:T(128)} %bitcast.23, f32[1,64,256]{2,1,0:T(8,128)S(1)} %get-tuple-element.48, ...), kind=kLoop, calls=%fused_computation.253 | loop fusion | flops 409600 | bytes 720916 | tf_op jit(solution)/shard_map/mul | solution.py:171
  71.1 3.3 %subtract_bitcast_fusion = (f32[64,256]{1,0:T(8,128)}, f32[1,64,256]{2,1,0:T(8,128)S(1)}, f32[1,64,256]{2,1,0:T(8,128)S(1)}) fusion(f32[]{:T(128)} %bitcast.47, f32[9,64,256]{2,1,0:T(8,128)S(1)} %slice_multiply_fusion.4, f32[]{:T(128)} %bitcast.43, f32[]{:T(128)} %bitcast.39, f32[1,64,256]{2,1,0:T(8,128)S(1)} %get-tuple-element.54, f32[]{:T(128)} %bitcast.35), kind=kLoop, calls=%fused_computation.186 | loop fusion | flops 409600 | bytes 458768 | tf_op jit(solution)/shard_map/div | solution.py:165
  74.4 5.4 %fusion.94 = (f32[64,256]{1,0:T(8,128)}, f32[64,256]{1,0:T(8,128)}, f32[64,256]{1,0:T(8,128)}, f32[64,256]{1,0:T(8,128)}, f32[64,256]{1,0:T(8,128)}, /*index=5*/...) fusion(f32[]{:T(128)} %bitcast.19, ...), kind=kLoop, calls=%fused_computation.239 | loop fusion | flops 327680 | bytes 1179676 | tf_op jit(solution)/shard_map/mul | solution.py:164
  81.1 3.3 %fusion.105 = (f32[64,256]{1,0:T(8,128)}, f32[64,256]{1,0:T(8,128)}, f32[64,256]{1,0:T(8,128)}, f32[64,256]{1,0:T(8,128)S(1)}) fusion(f32[1,64,256]{2,1,0:T(8,128)S(1)} %get-tuple-element.58, f32[]{:T(128)} %bitcast.39, f32[9,64,256]{2,1,0:T(8,128)S(1)} %slice_multiply_fusion.4, f32[1,64,256]{2,1,0:T(8,128)S(1)} %get-tuple-element.55, f32[]{:T(128)} %bitcast.31, ...), kind=kLoop, calls=%fused_computation.256 | loop fusion | flops 163840 | bytes 655376 | tf_op jit(solution)/shard_map/mul | solution.py:171
  84.4 2.5 %copy.96 = f32[5,10,64,1]{3,2,1,0:T(8,128)} copy(f32[5,10,64,1]{2,3,1,0:T(1,128)} %collective-permute-done) | data formatting | bytes 25600 | tf_op jit(solution)/shard_map/ppermute | solution.py:21
  86.9 2.5 %copy.97 = f32[5,10,64,1]{3,2,1,0:T(8,128)} copy(f32[5,10,64,1]{2,3,1,0:T(1,128)} %collective-permute-done.1) | data formatting | bytes 25600 | tf_op jit(solution)/shard_map/ppermute | solution.py:23
  89.3 2.4 %pad_maximum_fusion.4 = (f32[5,10,1,258]{3,2,1,0:T(1,128)}, f32[5,10,1,258]{3,2,1,0:T(1,128)}) fusion(f32[5,10,64,1]{3,2,1,0:T(8,128)} %copy.97, f32[5,10,64,256]{3,2,1,0:T(8,128)S(1)} %bitcast_dynamic-update-slice_fusion, f32[5,10,64,1]{3,2,1,0:T(8,128)} %copy.96), kind=kLoop, calls=%fused_computation.176 | loop fusion | flops 51600 | bytes 3405600 | tf_op jit(solution)/shard_map/slice | solution.py:18
  97.4 2.2 %collective-permute-done.3 = f32[5,10,1,258]{3,2,1,0:T(1,128)} collective-permute-done((f32[5,10,1,258]{3,2,1,0:T(1,128)}, f32[5,10,1,258]{3,2,1,0:T(1,128)}, u32[]{:S(2)}, u32[]{:S(2)}) %collective-permute-start.3) | collective-permute-done | bytes 51632 | tf_op jit(solution)/shard_map/ppermute | solution.py:23
  99.6 4.4 %fusion = f32[5,10,66,258]{3,2,1,0:T(8,128)S(1)} fusion(f32[5,10,1,258]{3,2,1,0:T(1,128)} %collective-permute-done.3, f32[5,10,64,1]{3,2,1,0:T(8,128)} %copy.97, f32[5,10,64,256]{3,2,1,0:T(8,128)S(1)} %bitcast_dynamic-update-slice_fusion, f32[5,10,64,1]{3,2,1,0:T(8,128)} %copy.96, f32[5,10,1,258]{3,2,1,0:T(1,128)} %collective-permute-done.2, ...), kind=kLoop, calls=%fused_computation.4 | loop fusion | flops 5108400 | bytes 6862932 | tf_op jit(solution)/shard_map/jit(_where)/select_n | solution.py:47
  111.0 6.0 %copy.108 = f32[1,10,64,256]{1,3,2,0:T(8,128)} copy(f32[1,10,64,256]{3,2,1,0:T(8,128)} %get-tuple-element.70) | data formatting | bytes 1310720
  117.1 6.0 %copy.109 = f32[1,10,64,256]{1,3,2,0:T(8,128)} copy(f32[1,10,64,256]{3,2,1,0:T(8,128)} %get-tuple-element.73) | data formatting | bytes 1310720
  123.0 11.8 %multiply_add_fusion = f32[1,10,64,256]{1,3,2,0:T(8,128)} fusion(f32[1,10,64,256]{1,3,2,0:T(8,128)} %copy.109, f32[1,10,64,256]{1,3,2,0:T(8,128)} %copy.108), kind=kLoop, calls=%fused_computation.2 | loop fusion | flops 491520 | bytes 1966080 | tf_op jit(solution)/shard_map/add | solution.py:204
  135.8 28.0 %all-gather.1 = f32[10,1,4096]{0,2,1:T(8,128)} all-gather(f32[10,1,256]{0,2,1:T(8,128)S(1)} %fusion.68), channel_id=3, replica_groups=mesh['lon'=16,'lat'=8] {'lon'}, dimensions={2}, use_global_device_ids=true | all-gather | bytes 174080 | tf_op jit(solution)/shard_map/all_gather | solution.py:207
  163.8 2.9 %gather_fusion.1 = f32[256,10]{1,0:T(8,128)} fusion(f32[10,4096]{0,1:T(8,128)} %bitcast.107, s32[1024]{0:T(1024)S(1)} %pad_clamp_fusion), kind=kCustom, calls=%fused_computation.1 | custom fusion | bytes 21504 | tf_op jit(solution)/shard_map/jit(_take)/gather | solution.py:209
  169.8 5.0 %collective-permute-start.5 = (f32[1,10,64,1]{1,3,2,0:T(1,128)}, f32[1,10,64,1]{1,3,2,0:T(1,128)}, u32[]{:S(2)}, u32[]{:S(2)}) collective-permute-start(f32[1,10,64,1]{1,3,2,0:T(1,128)} %get-tuple-element.60), channel_id=1, source_target_pairs={{8,0},{16,8},{24,16},{32,24},{40,32},{48,40},{56,48},{64,56},{72,6... | collective-permute-start | bytes 7688 | tf_op jit(solution)/shard_map/ppermute | solution.py:23
  175.4 6.0 %copy.102 = f32[1,10,64,256]{3,2,1,0:T(8,128)} copy(f32[1,10,64,256]{1,3,2,0:T(8,128)} %multiply_add_fusion) | data formatting | bytes 1310720 | tf_op jit(solution)/shard_map/add | solution.py:204
  192.1 3.1 %collective-permute-done.7 = f32[1,10,1,258]{3,2,1,0:T(1,128)S(1)} collective-permute-done((f32[1,10,1,258]{3,2,1,0:T(1,128)S(1)}, f32[1,10,1,258]{3,2,1,0:T(1,128)S(1)}, u32[]{:S(2)}, u32[]{:S(2)}) %collective-permute-start.7) | collective-permute-done | bytes 10352 | tf_op jit(solution)/shard_map/ppermute | solution.py:23
  (230 shorter events, 47.5 us)
Async XLA Ops:
  5.6 10.0 %copy-start.75 = (s32[256]{0:T(256)S(1)}, s32[256]{0:T(256)}, u32[]{:S(2)}) copy-start(s32[256]{0:T(256)} %param.20) | copy-start | bytes 3076
  7.5 76.8 %collective-permute-start = (f32[5,10,64,1]{2,3,1,0:T(1,128)S(1)}, f32[5,10,64,1]{2,3,1,0:T(1,128)}, u32[]{:S(2)}, u32[]{:S(2)}) collective-permute-start(f32[5,10,64,1]{2,3,1,0:T(1,128)S(1)} %copy.106), channel_id=1, source_target_pairs={{0,8},{8,16},{16,24},{24,32},{32,40},{40,48},{48,56},{56,64},{64,7... | collective-permute-start | bytes 38408 | tf_op jit(solution)/shard_map/ppermute | solution.py:21
  10.2 76.7 %collective-permute-start.1 = (f32[5,10,64,1]{2,3,1,0:T(1,128)}, f32[5,10,64,1]{2,3,1,0:T(1,128)}, u32[]{:S(2)}, u32[]{:S(2)}) collective-permute-start(f32[5,10,64,1]{2,3,1,0:T(1,128)} %copy.107), channel_id=1, source_target_pairs={{8,0},{16,8},{24,16},{32,24},{40,32},{48,40},{56,48},{64,56},{72,6... | collective-permute-start | bytes 38408 | tf_op jit(solution)/shard_map/ppermute | solution.py:23
  42.8 9.9 %copy-start.74 = (f32[10]{0:T(128)S(1)}, f32[10]{0:T(128)}, u32[]{:S(2)}) copy-start(f32[10]{0:T(128)} %param.17) | copy-start | bytes 124
  65.0 6.0 %copy-start.30 = (f32[1,64,256]{2,1,0:T(8,128)}, f32[1,64,256]{2,1,0:T(8,128)S(1)}, u32[]{:S(2)}) copy-start(f32[1,64,256]{2,1,0:T(8,128)S(1)} %get-tuple-element.48) | copy-start | bytes 196612
  65.0 9.4 %copy-start.33 = (f32[1,64,256]{2,1,0:T(8,128)}, f32[1,64,256]{2,1,0:T(8,128)S(1)}, u32[]{:S(2)}) copy-start(f32[1,64,256]{2,1,0:T(8,128)S(1)} %get-tuple-element.49) | copy-start | bytes 196612
  65.0 14.7 %copy-start.18 = (f32[256,5,10]{2,1,0:T(8,128)S(1)}, f32[256,5,10]{2,1,0:T(8,128)}, u32[]{:S(2)}) copy-start(f32[256,5,10]{2,1,0:T(8,128)} %gather_fusion) | copy-start | bytes 153604
  65.0 14.7 %copy-start.78 = (f32[5]{0:T(128)S(1)}, f32[5]{0:T(128)}, u32[]{:S(2)}) copy-start(f32[5]{0:T(128)} %constant.78.clone) | copy-start | bytes 64
  68.9 12.1 %copy-start.24 = (f32[1,64,256]{2,1,0:T(8,128)}, f32[1,64,256]{2,1,0:T(8,128)S(1)}, u32[]{:S(2)}) copy-start(f32[1,64,256]{2,1,0:T(8,128)S(1)} %get-tuple-element.52) | copy-start | bytes 196612
  71.0 3.3 %copy-start.39 = (f32[1,64,256]{2,1,0:T(8,128)}, f32[1,64,256]{2,1,0:T(8,128)S(1)}, u32[]{:S(2)}) copy-start(f32[1,64,256]{2,1,0:T(8,128)S(1)} %get-tuple-element.54) | copy-start | bytes 196612
  71.0 10.1 %copy-start.42 = (f32[1,64,256]{2,1,0:T(8,128)}, f32[1,64,256]{2,1,0:T(8,128)S(1)}, u32[]{:S(2)}) copy-start(f32[1,64,256]{2,1,0:T(8,128)S(1)} %get-tuple-element.55) | copy-start | bytes 196612
  74.4 6.7 %copy-start.19 = (f32[1,64,256]{2,1,0:T(8,128)}, f32[1,64,256]{2,1,0:T(8,128)S(1)}, u32[]{:S(2)}) copy-start(f32[1,64,256]{2,1,0:T(8,128)S(1)} %get-tuple-element.57) | copy-start | bytes 196612
  74.4 6.7 %copy-start.27 = (f32[1,64,256]{2,1,0:T(8,128)}, f32[1,64,256]{2,1,0:T(8,128)S(1)}, u32[]{:S(2)}) copy-start(f32[1,64,256]{2,1,0:T(8,128)S(1)} %get-tuple-element.58) | copy-start | bytes 196612
  89.3 6.5 %copy-start.76 = (f32[64]{0:T(128)S(1)}, f32[64]{0:T(128)}, u32[]{:S(2)}) copy-start(f32[64]{0:T(128)} %param.18) | copy-start | bytes 772
  91.7 5.6 %collective-permute-start.2 = (f32[5,10,1,258]{3,2,1,0:T(1,128)}, f32[5,10,1,258]{3,2,1,0:T(1,128)}, u32[]{:S(2)}, u32[]{:S(2)}) collective-permute-start(f32[5,10,1,258]{3,2,1,0:T(1,128)} %get-tuple-element.61), channel_id=1, source_target_pairs={{0,1},{1,2},{2,3},{3,4},{4,5},{5,6},{6,7},{7,0},{8,9},{9,10},{10,1... | collective-permute-start | bytes 154808 | tf_op jit(solution)/shard_map/ppermute | solution.py:21
  92.8 6.8 %collective-permute-start.3 = (f32[5,10,1,258]{3,2,1,0:T(1,128)}, f32[5,10,1,258]{3,2,1,0:T(1,128)}, u32[]{:S(2)}, u32[]{:S(2)}) collective-permute-start(f32[5,10,1,258]{3,2,1,0:T(1,128)} %get-tuple-element.62), channel_id=1, source_target_pairs={{1,0},{2,1},{3,2},{4,3},{5,4},{6,5},{7,6},{0,7},{9,8},{10,9},{11,1... | collective-permute-start | bytes 154808 | tf_op jit(solution)/shard_map/ppermute | solution.py:23
  106.0 2.5 %copy-start = (f32[10,64,256]{2,1,0:T(8,128)}, f32[10,64,256]{2,1,0:T(8,128)S(1)}, u32[]{:S(2)}) copy-start(f32[10,64,256]{2,1,0:T(8,128)S(1)} %get-tuple-element.75) | copy-start | bytes 1966084
  169.4 13.0 %collective-permute-start.4 = (f32[1,10,64,1]{1,3,2,0:T(1,128)}, f32[1,10,64,1]{1,3,2,0:T(1,128)}, u32[]{:S(2)}, u32[]{:S(2)}) collective-permute-start(f32[1,10,64,1]{1,3,2,0:T(1,128)} %get-tuple-element.59), channel_id=1, source_target_pairs={{0,8},{8,16},{16,24},{24,32},{32,40},{40,48},{48,56},{56,64},{64,7... | collective-permute-start | bytes 7688 | tf_op jit(solution)/shard_map/ppermute | solution.py:21
  169.8 14.7 %collective-permute-start.5 = (f32[1,10,64,1]{1,3,2,0:T(1,128)}, f32[1,10,64,1]{1,3,2,0:T(1,128)}, u32[]{:S(2)}, u32[]{:S(2)}) collective-permute-start(f32[1,10,64,1]{1,3,2,0:T(1,128)} %get-tuple-element.60), channel_id=1, source_target_pairs={{8,0},{16,8},{24,16},{32,24},{40,32},{48,40},{56,48},{64,56},{72,6... | collective-permute-start | bytes 7688 | tf_op jit(solution)/shard_map/ppermute | solution.py:23
  186.4 3.9 %copy-start.8 = (f32[1,10,64,256]{3,2,1,0:T(8,128)S(1)}, f32[1,10,64,256]{3,2,1,0:T(8,128)}, u32[]{:S(2)}) copy-start(f32[1,10,64,256]{3,2,1,0:T(8,128)} %copy.102) | copy-start | bytes 1966084
  186.4 3.9 %copy-start.9 = (f32[1,10,64,1]{3,2,1,0:T(8,128)S(1)}, f32[1,10,64,1]{3,2,1,0:T(8,128)}, u32[]{:S(2)}) copy-start(f32[1,10,64,1]{3,2,1,0:T(8,128)} %copy.101) | copy-start | bytes 7684
  186.4 3.9 %copy-start.10 = (f32[1,10,64,1]{3,2,1,0:T(8,128)S(1)}, f32[1,10,64,1]{3,2,1,0:T(8,128)}, u32[]{:S(2)}) copy-start(f32[1,10,64,1]{3,2,1,0:T(8,128)} %copy.103) | copy-start | bytes 7684
  188.3 3.8 %collective-permute-start.6 = (f32[1,10,1,258]{3,2,1,0:T(1,128)S(1)}, f32[1,10,1,258]{3,2,1,0:T(1,128)S(1)}, u32[]{:S(2)}, u32[]{:S(2)}) collective-permute-start(f32[1,10,1,258]{3,2,1,0:T(1,128)S(1)} %get-tuple-element.87), channel_id=1, source_target_pairs={{0,1},{1,2},{2,3},{3,4},{4,5},{5,6},{6,7},{7,0},{8,9},{9,10},{10,1... | collective-permute-start | bytes 30968 | tf_op jit(solution)/shard_map/ppermute | solution.py:21
  189.3 5.8 %collective-permute-start.7 = (f32[1,10,1,258]{3,2,1,0:T(1,128)S(1)}, f32[1,10,1,258]{3,2,1,0:T(1,128)S(1)}, u32[]{:S(2)}, u32[]{:S(2)}) collective-permute-start(f32[1,10,1,258]{3,2,1,0:T(1,128)S(1)} %get-tuple-element.88), channel_id=1, source_target_pairs={{1,0},{2,1},{3,2},{4,3},{5,4},{6,5},{7,6},{0,7},{9,8},{10,9},{11,1... | collective-permute-start | bytes 30968 | tf_op jit(solution)/shard_map/ppermute | solution.py:23
  (63 other events, 124.1 us)
where the time goes:
time: 205 us; the launch traced here: 203 us
  local copies, waits for them, and re-layouts  69.1 us (34%)
  other arithmetic  57.6 us (28%)
  blocking collectives  52.5 us (26%)
  starting transfers between devices  14.9 us (7%)
  waiting for transfers between devices  6.63 us (3%)
  between operations  2.52 us (1%)
    all_gather x1, blocking collectives, on_device(): gathered_density = lax.all_gather(density_rows, 'lon', axis=2, tiled=True)  28 us
    all_gather x1, blocking collectives, on_device(): gathered = lax.all_gather(fold_rows, 'lon', axis=2, tiled=True)  24.6 us
    unnamed x175, local copies, waits for them, and re-layouts  23.5 us
    add x2, other arithmetic, on_device(): -thermal_coeff * new_tracers[0] + haline_coeff * new_tracers[1]  12.8 us
    ppermute x4, starting transfers between devices, padded_2(): lax.ppermute(head, axis, [((i + 1) % count, i) for i in range(count)])  12.3 us
    mul x4, other arithmetic, solve_columns(): after = forward[layer] - bands[layer][2] * after  11.8 us
    all_gather x1, local copies, waits for them, and re-layouts, on_device(): gathered = lax.all_gather(fold_rows, 'lon', axis=2, tiled=True)  9.89 us
    gather x1, local copies, waits for them, and re-layouts, on_device(): ghost_row = jnp.take(gathered, seam_partner_meridian, axis=2)  7.5 us
  transfers between devices with their start and end apart: 8, of which 3 were waited for; matrix products, arithmetic and copies ran while one was open for 31% of the time, Pallas kernels for 0%

commit v1 on v0

v1 whole, which is shorter than its diff:
```python
import functools

import jax
import jax.numpy as jnp
from jax import lax
from jax.experimental import pallas as pl
from jax.experimental.pallas import tpu as pltpu
from jax.sharding import PartitionSpec as P

LEVELS = 10
ROWS = 64
COLS = 256
TILE = 8
LANES = 128
HEAT, SALT, EAST, NORTH, WET, PART, MIX = 0, 10, 20, 30, 40, 50, 60
PAYLOAD = 72
SOUTH_LANE, NORTH_LANE = 64, 65
F_ROW = 40
EAST_SIDE = 48
GRAIN = 0.06


def iota(shape, dim):
    return lax.broadcasted_iota(jnp.int32, shape, dim)


def weights(wet_a, wet_b, speed_a, speed_b):
    both = wet_a * wet_b
    speed = 0.1 * (speed_a + speed_b)
    return both * (jnp.maximum(speed, 0.0) + GRAIN), both * (jnp.minimum(speed, 0.0) - GRAIN)


def east_of(x):
    return pltpu.roll(x, x.shape[1] - 1, 1)


def west_of(x):
    return pltpu.roll(x, 1, 1)


def north_of(x, block_above, sub):
    return pltpu.roll(jnp.where(sub == 0, block_above, x), TILE - 1, 0)


def south_of(x, block_below, sub):
    return pltpu.roll(jnp.where(sub == TILE - 1, block_below, x), 1, 0)


def mix_down(heat, salt):
    return 0.8 * salt - 0.2 * heat


def pack_rows(hinge_ref, *refs):
    bottom, top, (a_ref, b_ref) = refs[:6], refs[6:12], refs[12:]
    lat = lax.axis_index("lat")
    at_top = lat == lax.axis_size("lat") - 1
    even = lat % 2 == 0
    hinged = jnp.logical_and(at_top, hinge_ref[0] == 1)
    inner = (iota((TILE, COLS), 1) < COLS - 1).astype(jnp.float32)
    sub = iota((TILE, COLS), 0)
    for level in range(LEVELS):
        sides = []
        for heat_ref, salt_ref, east_ref, north_ref, wet_ref, mix_ref in (bottom, top):
            heat, salt = heat_ref[level], salt_ref[level]
            east, north = east_ref[level], north_ref[level]
            wet = wet_ref[level].astype(jnp.float32)
            mixed = mix_down(heat, salt)
            here, there = weights(wet * inner, east_of(wet), east, east_of(east))
            flux_e = here * mixed + there * east_of(mixed)
            above = lambda x: pltpu.roll(x, TILE - 1, 0)
            here, there = weights(wet, above(wet), north, above(north))
            flux_n = here * mixed + there * above(mixed)
            part = mixed - (flux_e - west_of(flux_e))
            sides.append((heat, salt, east, north, wet, part, mix_ref[min(level, LEVELS - 2)], flux_n))
        *low, flux_n = sides[0]
        low[5] = low[5] - flux_n
        low = [x[:1] for x in low]
        *high, flux_n = sides[1]
        flux_s = pltpu.roll(flux_n, 1, 0)
        high[5] = high[5] + flux_s - jnp.where(sub == TILE - 1, 0.0, flux_n)
        high = [jnp.where(hinged, x[TILE - 2 : TILE - 1], x[TILE - 1 :]) for x in high]
        for start, one, other in zip((HEAT, SALT, EAST, NORTH, WET, PART, MIX), low, high):
            if start == MIX and level == LEVELS - 1:
                continue
            a_ref[start + level : start + level + 1] = jnp.where(even, other, one)
            b_ref[start + level : start + level + 1] = jnp.where(even, one, other)
    for ref in (a_ref, b_ref):
        ref[MIX + LEVELS - 1 :] = jnp.zeros((PAYLOAD - MIX - LEVELS + 1, COLS), jnp.float32)

    @pl.when(at_top)
    def _():
        back = LANES - 1 - iota((TILE, LANES), 1)
        for row in range(0, PAYLOAD, TILE):
            place = row + iota((TILE, LANES), 0)
            sign = jnp.where(jnp.logical_and(place >= EAST, place < WET), -1.0, 1.0)
            left = b_ref[row : row + TILE, :LANES]
            right = b_ref[row : row + TILE, LANES:]
            flip = lambda x: sign * jnp.take_along_axis(x, back, axis=1, mode="promise_in_bounds")
            b_ref[row : row + TILE, :LANES] = flip(right)
            b_ref[row : row + TILE, LANES:] = flip(left)


def from_lat(a_ref, b_ref):
    even = lax.axis_index("lat") % 2 == 0
    a, b = a_ref[...], b_ref[...]
    return jnp.where(even, b, a), jnp.where(even, a, b)


def load(pairs, sems):
    copies = [pltpu.make_async_copy(src, dst, sems.at[i]) for i, (src, dst) in enumerate(pairs)]
    for copy in copies:
        copy.start()
    return copies


def advect(
    hinge_ref, heat_ref, salt_ref, east_ref, north_ref, wet_ref, mix_ref, a_ref, b_ref,
    heat_out, salt_out, rhs_out, c_out, d_out,
    heat_x, salt_x, east_x, north_x, wet_x, mix_x, heat_f, salt_f, rim, ghost, sems,
):
    inside = pl.ds(TILE, ROWS)
    copies = load(
        [
            (heat_ref, heat_x.at[:, inside]),
            (salt_ref, salt_x.at[:, inside]),
            (east_ref, east_x),
            (north_ref, north_x.at[:, inside]),
            (wet_ref, wet_x.at[:, inside]),
            (mix_ref, mix_x),
        ],
        sems,
    )
    lat = lax.axis_index("lat")
    at_top = lat == lax.axis_size("lat") - 1
    open_north = jnp.where(jnp.logical_and(at_top, hinge_ref[0] == 1), 0.0, 1.0)
    ghost[0], ghost[1] = from_lat(a_ref, b_ref)
    inner = (iota((TILE, COLS), 1) < COLS - 1).astype(jnp.float32)
    sub = iota((TILE, COLS), 0)
    lane = iota((TILE, LANES), 1)
    south_row, north_row = TILE - 1, TILE + ROWS
    for level in range(LEVELS):
        for ref, start in ((heat_x, HEAT), (salt_x, SALT), (north_x, NORTH), (wet_x, WET)):
            for side, row in ((0, south_row), (1, north_row)):
                ref[level, row : row + 1] = ghost[side, start + level : start + level + 1].astype(ref.dtype)
    for copy in copies:
        copy.wait()

    def north_faces(level, block):
        rows = pl.ds(pl.multiple_of(block * TILE, TILE), TILE)
        above = pl.ds(pl.multiple_of(block * TILE + TILE, TILE), TILE)
        pick = lambda ref: (ref[level, rows], north_of(ref[level, rows], ref[level, above], sub))
        heat, heat_n = pick(heat_x)
        salt, salt_n = pick(salt_x)
        north, north_n = pick(north_x)
        wet, wet_n = (x.astype(jnp.float32) for x in pick(wet_x))
        here, there = weights(wet, wet_n, north, north_n)
        return heat, salt, wet, here * heat + there * heat_n, here * salt + there * salt_n

    for level in range(LEVELS):
        _, _, _, heat_n, salt_n = north_faces(level, 0)
        heat_f[level], salt_f[level] = heat_n, salt_n
        flux = mix_down(heat_n, salt_n)[TILE - 1 :]
        rhs_out[16 + level : 17 + level] = ghost[0, PART + level : PART + level + 1] - flux

    def step(block, _):
        rows = pl.ds(pl.multiple_of(block * TILE, TILE), TILE)
        west_rim = jnp.zeros((TILE, LANES), jnp.float32)
        east_rim = west_rim
        for level in range(LEVELS):
            heat, salt, wet, heat_n, salt_n = north_faces(level, block + 1)
            east = east_x[level, rows]
            heat_s = south_of(heat_n, heat_f[level], sub)
            salt_s = south_of(salt_n, salt_f[level], sub)
            heat_f[level], salt_f[level] = heat_n, salt_n
            here, there = weights(wet * inner, east_of(wet), east, east_of(east))
            heat_e = here * heat + there * east_of(heat)
            salt_e = here * salt + there * east_of(salt)
            new_heat = heat - ((heat_e - west_of(heat_e)) + (heat_n - heat_s))
            new_salt = salt - ((salt_e - west_of(salt_e)) + (salt_n - salt_s))
            heat_out[level, rows] = new_heat
            salt_out[level, rows] = new_salt
            fields = [
                (HEAT, heat),
                (SALT, salt),
                (EAST, east),
                (NORTH, north_x[level, pl.ds(pl.multiple_of(block * TILE + TILE, TILE), TILE)]),
                (WET, wet),
                (PART, mix_down(new_heat, new_salt)),
            ]
            if level < LEVELS - 1:
                fields.append((MIX, mix_x[level, rows]))
            for start, x in fields:
                place = start + level
                west_rim = jnp.where(lane == place, pltpu.roll(x[:, :LANES], place, 1), west_rim)
                east_rim = jnp.where(lane == place, pltpu.roll(x[:, LANES:], place + 1, 1), east_rim)
        rim[0, rows] = west_rim
        rim[1, rows] = east_rim
        return 0

    lax.fori_loop(0, ROWS // TILE, step, 0)
    for level in range(LEVELS):
        flux = mix_down(heat_f[level], salt_f[level])[TILE - 1 :]
        rhs_out[level : level + 1] = ghost[1, PART + level : PART + level + 1] + open_north * flux
    sides = []
    wide = iota((PAYLOAD, LANES), 1)
    for side, column in ((0, 0), (1, COLS - 1)):
        turned = jnp.transpose(rim[side])[:PAYLOAD]
        turned = jnp.where(wide < ROWS, turned, 0.0)
        for place, which in ((SOUTH_LANE, 0), (NORTH_LANE, 1)):
            turned = jnp.where(wide == place, ghost[which, :, column : column + 1], turned)
        sides.append(turned)
    even = lax.axis_index("lon") % 2 == 0
    c_out[...] = jnp.where(even, sides[1], sides[0])
    d_out[...] = jnp.where(even, sides[0], sides[1])


def factor(thick, mix, wet):
    inverse, weight, ratio = [], [], []
    for level in range(LEVELS):
        diagonal = thick[level]
        if level < LEVELS - 1:
            weight.append((0.2 * mix[level]) * (wet[level] * wet[level + 1]))
            diagonal = diagonal + weight[level]
        if level > 0:
            diagonal = diagonal + weight[level - 1] * (1.0 - ratio[level - 1])
        inverse.append(1.0 / diagonal)
        if level < LEVELS - 1:
            ratio.append(weight[level] * inverse[level])
    return inverse, weight, ratio


def solve(thick, inverse, weight, ratio, right):
    x = []
    for level in range(LEVELS):
        now = thick[level] * right[level]
        if level > 0:
            now = now + weight[level - 1] * x[level - 1]
        x.append(now * inverse[level])
    for level in reversed(range(LEVELS - 1)):
        x[level] = x[level] + ratio[level] * x[level + 1]
    return x


def pressures(thick, density):
    above, out = None, []
    for level in range(LEVELS):
        layer = (0.1 * thick[level]) * density[level]
        out.append(0.5 * layer if above is None else above + 0.5 * layer)
        above = layer if above is None else above + layer
    return out


def finish(
    thick_ref, spin_ref, heat_ref, salt_ref, east_ref, north_ref, wet_ref, mix_ref,
    a_ref, b_ref, rhs_ref, c_own_ref, d_own_ref, c_ref, d_ref,
    heat_out, salt_out, east_out, north_out,
    east_x, north_x, wet_x, mix_x, press_x, inv_x, weight_x, ghost, rims,
    rim_rhs, rim_mix, rim_wet, rim_press, rim_rows, fixes, east_f, north_f, sems,
):
    inside = pl.ds(TILE, ROWS)
    copies = load(
        [
            (east_ref, east_x.at[:, inside]),
            (north_ref, north_x.at[:, inside]),
            (wet_ref, wet_x.at[:, inside]),
            (mix_ref, mix_x),
        ],
        sems,
    )
    thick = [thick_ref[level] for level in range(LEVELS)]
    ghost[0], ghost[1] = from_lat(a_ref, b_ref)
    even = lax.axis_index("lon") % 2 == 0
    rims[0] = jnp.where(even, d_own_ref[...], c_own_ref[...])
    rims[1] = jnp.where(even, d_ref[...], c_ref[...])
    rims[2] = jnp.where(even, c_own_ref[...], d_own_ref[...])
    rims[3] = jnp.where(even, c_ref[...], d_ref[...])
    south_row, north_row = TILE - 1, TILE + ROWS
    for level in range(LEVELS):
        for ref, start in ((east_x, EAST), (north_x, NORTH), (wet_x, WET)):
            for side, row in ((0, south_row), (1, north_row)):
                ref[level, row : row + 1] = ghost[side, start + level : start + level + 1].astype(ref.dtype)

    span = lambda which, start: rims[which, start : start + LEVELS]
    lane = iota((LEVELS, LANES), 1)
    mixed_flux = []
    for side, (left, right) in enumerate(((1, 0), (2, 3))):
        here, there = weights(span(left, WET), span(right, WET), span(left, EAST), span(right, EAST))
        heat_e = here * span(left, HEAT) + there * span(right, HEAT)
        salt_e = here * span(left, SALT) + there * span(right, SALT)
        own = 1.0 if side == 0 else -1.0
        base = side * EAST_SIDE
        fixes[base : base + LEVELS] = own * heat_e
        fixes[base + LEVELS : base + 2 * LEVELS] = own * salt_e
        mixed_flux.append(own * mix_down(heat_e, salt_e))
    rim_rows[0:LEVELS] = span(0, PART) + mixed_flux[0]
    rim_rows[16 : 16 + LEVELS] = span(1, PART) - mixed_flux[0]
    rim_rows[32 : 32 + LEVELS] = span(2, PART) + mixed_flux[1]
    rim_rows[48 : 48 + LEVELS] = span(3, PART) - mixed_flux[1]
    for side, (start, end) in ((1, (0, NORTH_LANE)), (0, (16, SOUTH_LANE))):
        low = rhs_ref[start : start + LEVELS, :LANES]
        high = rhs_ref[start : start + LEVELS, LANES:]
        low = low + jnp.where(lane == 0, mixed_flux[0][:, end : end + 1], 0.0)
        high = high + jnp.where(lane == LANES - 1, mixed_flux[1][:, end : end + 1], 0.0)
        base = 64 + 32 * (1 - side)
        rim_rows[base : base + LEVELS] = low
        rim_rows[base + 16 : base + 16 + LEVELS] = high
    for level in range(LEVELS):
        for slot in range(TILE):
            rim_rhs[level, slot : slot + 1] = rim_rows[16 * slot + level : 16 * slot + level + 1]
            for ref, start in ((rim_mix, MIX), (rim_wet, WET)):
                row = slice(start + level, start + level + 1)
                if slot < 4:
                    value = rims[slot, row]
                else:
                    half = (slot % 2) * LANES
                    value = ghost[1 - (slot - 4) // 2, row, half : half + LANES]
                ref[level, slot : slot + 1] = value
    listed = lambda ref: [ref[level] for level in range(LEVELS)]
    bands = factor(thick, listed(rim_mix), listed(rim_wet))
    rim_density = solve(thick, *bands, listed(rim_rhs))
    for level, value in enumerate(pressures(thick, rim_density)):
        rim_press[level] = value
        for slot in range(4):
            rim_rows[16 * slot + level : 16 * slot + level + 1] = rim_press[level, slot : slot + 1]
        press_x[level, north_row : north_row + 1, :LANES] = rim_press[level, 4:5]
        press_x[level, north_row : north_row + 1, LANES:] = rim_press[level, 5:6]
        press_x[level, south_row : south_row + 1, :LANES] = rim_press[level, 6:7]
        press_x[level, south_row : south_row + 1, LANES:] = rim_press[level, 7:8]
    for side, (left, right) in enumerate(((1, 0), (2, 3))):
        both = span(left, WET) * span(right, WET)
        own = -1.0 if side == 0 else 1.0
        slope = 0.1 * both * (
            rim_rows[16 * right : 16 * right + LEVELS] - rim_rows[16 * left : 16 * left + LEVELS]
        )
        base = side * EAST_SIDE + 2 * LEVELS
        fixes[base : base + LEVELS] = own * GRAIN * both * (span(right, EAST) - span(left, EAST)) - slope
        fixes[base + LEVELS : base + 2 * LEVELS] = own * GRAIN * both * (span(right, NORTH) - span(left, NORTH))
    fixes[F_ROW : F_ROW + 1, :ROWS] = 0.2 * spin_ref[...]
    fixes[...] = jnp.transpose(fixes[...])

    for copy in copies:
        copy.wait()
    sub = iota((TILE, COLS), 0)
    lanes = iota((TILE, LANES), 1)
    inner = (iota((TILE, COLS), 1) < COLS - 1).astype(jnp.float32)

    def fix(corner, which, level):
        place = which * LEVELS + level
        west = jnp.where(lanes == 0, pltpu.roll(corner, (LANES - place) % LANES, 1), 0.0)
        place = place + EAST_SIDE
        east = jnp.where(lanes == LANES - 1, pltpu.roll(corner, LANES - 1 - place, 1), 0.0)
        return jnp.concatenate([west, east], axis=1)

    def tracers(block, _):
        rows = pl.ds(pl.multiple_of(block * TILE, TILE), TILE)
        rows_x = pl.ds(pl.multiple_of(block * TILE + TILE, TILE), TILE)
        corner = fixes[rows]
        wet = [wet_x[level, rows_x].astype(jnp.float32) for level in range(LEVELS)]
        mix = [mix_x[level, rows] for level in range(LEVELS - 1)]
        inverse, weight, ratio = factor(thick, mix, wet)
        for level in range(LEVELS):
            inv_x[level, rows] = inverse[level]
            if level < LEVELS - 1:
                weight_x[level, rows] = weight[level]
        heat = [heat_ref[level, rows] + fix(corner, 0, level) for level in range(LEVELS)]
        salt = [salt_ref[level, rows] + fix(corner, 1, level) for level in range(LEVELS)]
        heat = solve(thick, inverse, weight, ratio, heat)
        salt = solve(thick, inverse, weight, ratio, salt)
        density = [mix_down(h, s) for h, s in zip(heat, salt)]
        for level, value in enumerate(pressures(thick, density)):
            heat_out[level, rows] = heat[level]
            salt_out[level, rows] = salt[level]
            press_x[level, rows_x] = value
        return 0

    lax.fori_loop(0, ROWS // TILE, tracers, 0)

    def north_faces(level, block):
        rows = pl.ds(pl.multiple_of(block * TILE, TILE), TILE)
        above = pl.ds(pl.multiple_of(block * TILE + TILE, TILE), TILE)
        pick = lambda ref: (ref[level, rows], north_of(ref[level, rows], ref[level, above], sub))
        east, east_n = pick(east_x)
        north, north_n = pick(north_x)
        press, press_n = pick(press_x)
        wet, wet_n = (x.astype(jnp.float32) for x in pick(wet_x))
        both = wet * wet_n
        spread = GRAIN * both
        slope = (0.1 * both) * (press_n - press)
        return east, north, press, wet, spread * (east_n - east), spread * (north_n - north), slope

    for level in range(LEVELS):
        *_, lap_east, lap_north, slope = north_faces(level, 0)
        east_f[level] = lap_east
        north_f[level] = lap_north + slope

    def flow(block, _):
        rows = pl.ds(pl.multiple_of(block * TILE, TILE), TILE)
        corner = fixes[rows]
        spin = jnp.broadcast_to(corner[:, F_ROW : F_ROW + 1], (TILE, COLS))
        new_east, new_north = [], []
        for level in range(LEVELS):
            east, north, press, wet, lap_east, lap_north, slope = north_faces(level, block + 1)
            from_south = south_of(lap_east, east_f[level], sub)
            push_south = south_of(lap_north + slope, north_f[level], sub)
            east_f[level] = lap_east
            north_f[level] = lap_north + slope
            both = wet * inner * east_of(wet)
            spread = GRAIN * both
            lap_east_e = spread * (east_of(east) - east)
            lap_north_e = spread * (east_of(north) - north)
            slope_e = (0.1 * both) * (east_of(press) - press)
            turn = wet * spin
            new_east.append(
                east + turn * north + (lap_east_e - slope_e) - west_of(lap_east_e + slope_e)
                + (lap_east - from_south) + fix(corner, 2, level)
            )
            new_north.append(
                north - turn * east + (lap_north_e - west_of(lap_north_e))
                + (lap_north - slope) - push_south + fix(corner, 3, level)
            )
        inverse = [inv_x[level, rows] for level in range(LEVELS)]
        weight = [weight_x[level, rows] for level in range(LEVELS - 1)]
        ratio = [weight[level] * inverse[level] for level in range(LEVELS - 1)]
        for out, right in ((east_out, new_east), (north_out, new_north)):
            for level, value in enumerate(solve(thick, inverse, weight, ratio, right)):
                out[level, rows] = value
        return 0

    lax.fori_loop(0, ROWS // TILE, flow, 0)


def swap_in_pairs(x, axis, first):
    count = lax.axis_size(axis)
    return lax.ppermute(x, axis, [(i, (((i - first) ^ 1) + first) % count) for i in range(count)])


def swap_with_fold(x, anchor):
    lon, lat = lax.axis_size("lon"), lax.axis_size("lat")
    pairs = []
    for i in range(lon):
        for j in range(1, lat - 1):
            pairs.append((i * lat + j, i * lat + ((j - 1) ^ 1) + 1))
        pairs.append((i * lat + lat - 1, (anchor - 1 - i) % lon * lat + lat - 1))
    return lax.ppermute(x, ("lon", "lat"), pairs)


def on_device(heat, salt, east, north, marine, mixing, spacing, spin, hinge, partner):
    f32, i32 = jnp.float32, jnp.int32
    lon = lax.axis_size("lon")
    anchor = (partner[0] + 1 + COLS * lax.axis_index("lon")) // COLS % lon
    smem = pl.BlockSpec(memory_space=pltpu.SMEM)
    vmem = pl.BlockSpec(memory_space=pltpu.VMEM)
    anywhere = pl.BlockSpec(memory_space=pl.ANY)
    shape = jax.ShapeDtypeStruct
    cells = (heat, salt, east, north, marine, mixing)
    edge = [
        pl.BlockSpec((x.shape[0], TILE, COLS), lambda i, at=at: (0, at, 0))
        for at in (0, ROWS // TILE - 1)
        for x in cells
    ]
    a_sent, b_sent = pl.pallas_call(
        pack_rows,
        grid=(1,),
        in_specs=[smem] + edge,
        out_specs=[pl.BlockSpec((PAYLOAD, COLS), lambda i: (0, 0))] * 2,
        out_shape=[shape((PAYLOAD, COLS), f32)] * 2,
        name="pack_rows",
    )(hinge, *cells, *cells)
    a_got = swap_in_pairs(a_sent, "lat", 0)
    b_got = lax.switch(anchor, [functools.partial(swap_with_fold, anchor=k) for k in range(lon)], b_sent)
    wide = (LEVELS, ROWS + 2 * TILE, COLS)
    plain = (LEVELS, ROWS, COLS)
    heat_step, salt_step, rhs, c_sent, d_sent = pl.pallas_call(
        advect,
        in_specs=[smem] + [anywhere] * 6 + [vmem] * 2,
        out_specs=[vmem] * 5,
        out_shape=[shape(plain, f32)] * 2 + [shape((32, COLS), f32)] + [shape((PAYLOAD, LANES), f32)] * 2,
        scratch_shapes=[
            pltpu.VMEM(wide, f32),
            pltpu.VMEM(wide, f32),
            pltpu.VMEM(plain, f32),
            pltpu.VMEM(wide, f32),
            pltpu.VMEM(wide, i32),
            pltpu.VMEM((LEVELS - 1, ROWS, COLS), f32),
            pltpu.VMEM((LEVELS, TILE, COLS), f32),
            pltpu.VMEM((LEVELS, TILE, COLS), f32),
            pltpu.VMEM((2, LANES, LANES), f32),
            pltpu.VMEM((2, PAYLOAD, COLS), f32),
            pltpu.SemaphoreType.DMA((6,)),
        ],
        compiler_params=pltpu.CompilerParams(vmem_limit_bytes=40 * 2**20),
        name="advect",
    )(hinge, *cells, a_got, b_got)
    c_got = swap_in_pairs(c_sent, "lon", 0)
    d_got = swap_in_pairs(d_sent, "lon", 1)
    return pl.pallas_call(
        finish,
        in_specs=[smem] + [vmem] * 3 + [anywhere] * 4 + [vmem] * 7,
        out_specs=[vmem] * 4,
        out_shape=[shape(plain, f32)] * 4,
        scratch_shapes=[
            pltpu.VMEM(wide, f32),
            pltpu.VMEM(wide, f32),
            pltpu.VMEM(wide, i32),
            pltpu.VMEM((LEVELS - 1, ROWS, COLS), f32),
            pltpu.VMEM(wide, f32),
            pltpu.VMEM(plain, f32),
            pltpu.VMEM(plain, f32),
            pltpu.VMEM((2, PAYLOAD, COLS), f32),
            pltpu.VMEM((4, PAYLOAD, LANES), f32),
            pltpu.VMEM((LEVELS, TILE, LANES), f32),
            pltpu.VMEM((LEVELS, TILE, LANES), f32),
            pltpu.VMEM((LEVELS, TILE, LANES), f32),
            pltpu.VMEM((LEVELS, TILE, LANES), f32),
            pltpu.VMEM((LANES, LANES), f32),
            pltpu.VMEM((LANES, LANES), f32),
            pltpu.VMEM((LEVELS, TILE, COLS), f32),
            pltpu.VMEM((LEVELS, TILE, COLS), f32),
            pltpu.SemaphoreType.DMA((4,)),
        ],
        compiler_params=pltpu.CompilerParams(vmem_limit_bytes=48 * 2**20),
        name="finish",
    )(
        spacing, spin.reshape(1, -1), heat_step, salt_step, east, north, marine, mixing,
        a_got, b_got, rhs, c_sent, d_sent, c_got, d_got,
    )


def solution(mesh):
    cells = P(None, "lat", "lon")
    return jax.shard_map(
        on_device,
        mesh=mesh,
        in_specs=(cells,) * 6 + (P(), P("lat"), P(), P("lon")),
        out_specs=(cells,) * 4,
        check_vma=False,
    )
```

time: 205 us -> 38.5 us (0.19)
  local copies, waits for them, and re-layouts: 69.1 us -> 2.96 us
  other arithmetic: 57.6 us -> 0 us
  blocking collectives: 52.5 us -> 0 us
  Pallas kernels: 0 us -> 16.2 us
  starting transfers between devices: 14.9 us -> 12.1 us
    all_gather x2 -> x0, blocking collectives: 52.5 us -> none  [the longest x1 28 us: on_device(): gathered_density = lax.all_gather(density_rows, 'lon', axis=2, tiled=True)]
    mul x8 -> x0, other arithmetic: 21.4 us -> none  [the longest x4 11.8 us: solve_columns(): after = forward[layer] - bands[layer][2] * after]
    unnamed x175 -> x18, local copies, waits for them, and re-layouts: 23.5 us -> 2.45 us
    pallas_call x0 -> x3, Pallas kernels: none -> 16.2 us  [the longest x1 6.83 us: on_device(): pl.pallas_call(finish, in_specs=[smem] + [vmem] * 3 + [anywhere] * 4 + [v...]
    add x2 -> x0, other arithmetic: 12.8 us -> none  [on_device(): -thermal_coeff * new_tracers[0] + haline_coeff * new_tracers[1]]
    gather x2 -> x0, local copies, waits for them, and re-layouts: 10.4 us -> none  [the longest x1 7.5 us: on_device(): ghost_row = jnp.take(gathered, seam_partner_meridian, axis=2)]
    all_gather x1 -> x0, local copies, waits for them, and re-layouts: 9.89 us -> none  [on_device(): gathered = lax.all_gather(fold_rows, 'lon', axis=2, tiled=True)]
    ppermute x4 -> x0, local copies, waits for them, and re-layouts: 8.95 us -> none  [the longest x2 4.49 us: padded_2(): lax.ppermute(tail, axis, [(i, (i + 1) % count) for i in range(count)])]
  transfers between devices with their start and end apart: 8 -> 4, of which waited for: 3 -> 2; matrix products, arithmetic and copies ran while one was open for 31% -> 1% of each run, Pallas kernels for 0% -> 0%
where the time goes in v1:
time: 38.5 us; the launch traced here: 38.1 us
  Pallas kernels  16.2 us (42%)
  starting transfers between devices  12.1 us (31%)
  waiting for transfers between devices  4.81 us (12%)
  local copies, waits for them, and re-layouts  2.96 us (8%)
  between operations  2.06 us (5%)
    ppermute x3, starting transfers between devices, swap_in_pairs(): lax.ppermute(x, axis, [(i, ((i - first ^ 1) + first) % count) for i in ra...  9.08 us
    pallas_call x1, Pallas kernels, on_device(): pl.pallas_call(finish, in_specs=[smem] + [vmem] * 3 + [anywhere] * 4 + [v...  6.83 us
    pallas_call x1, Pallas kernels, on_device(): pl.pallas_call(advect, in_specs=[smem] + [anywhere] * 6 + [vmem] * 2, out...  6.78 us
    ppermute x1, waiting for transfers between devices, swap_with_fold(): return lax.ppermute(x, ('lon', 'lat'), pairs)  3.17 us
    ppermute x1, starting transfers between devices, swap_with_fold(): return lax.ppermute(x, ('lon', 'lat'), pairs)  2.99 us
    pallas_call x1, Pallas kernels, on_device(): pl.pallas_call(pack_rows, grid=(1,), in_specs=[smem] + edge, out_specs=[p...  2.56 us
    unnamed x18, local copies, waits for them, and re-layouts  2.45 us
    ppermute x3, waiting for transfers between devices, swap_in_pairs(): lax.ppermute(x, axis, [(i, ((i - first ^ 1) + first) % count) for i in ra...  1.64 us
  transfers between devices with their start and end apart: 4, of which 2 were waited for; matrix products, arithmetic and copies ran while one was open for 1% of the time, Pallas kernels for 0%

profile of v1, /device:TPU:26, one launch (start us, length us, event | category | flops | bytes accessed | tf_op | source)
XLA Modules:
  0.0 38.1 jit_solution(2273976417072637474)
XLA Ops:
  1.3 0.0 copy-start
  1.3 0.0 copy-start.1
  1.3 0.0 copy-start.2
  1.3 0.0 copy-start.3
  1.3 0.0 copy-start.4
  1.3 2.6 %pack_rows.1 = (f32[72,256]{1,0:T(8,128)}, f32[72,256]{1,0:T(8,128)S(1)}) custom-call(s32[1]{0:T(128)S(6)} %copy.30.hinge_ref, f32[10,64,256]{2,1,0:T(8,128)} %heat_ref.1, f32[10,64,256]{2,1,0:T(8,128)} %salt_ref.1, f32[10,64,256]{2,1,0:T(8,128)} %east_ref.3, f32[10,64,256]{2,1,0:T(8,128)} %north_ref.3, s32[10,64,256]{2,1,0:T(8,128)} %wet_ref.3, ...), custom_call_target="tpu_custom_call" | custom-call | tf_op jit(solution)/shard_map/pack_rows/pallas_call | solution.py:461
  3.9 0.4 %collective-permute-start.16 = (f32[72,256]{1,0:T(8,128)}, f32[72,256]{1,0:T(8,128)S(1)}, u32[]{:S(2)}, u32[]{:S(2)}) collective-permute-start(f32[72,256]{1,0:T(8,128)} %get-tuple-element.44), channel_id=1, source_target_pairs={{0,1},{1,0},{2,3},{3,2},{4,5},{5,4},{6,7},{7,6},{8,9},{9,8},{10,11... | collective-permute-start | bytes 221192 | tf_op jit(solution)/shard_map/ppermute | solution.py:434
  4.3 0.7 %copy-done.8 = s32[256]{0:T(256)S(1)} copy-done((s32[256]{0:T(256)S(1)}, s32[256]{0:T(256)}, u32[]{:S(2)}) %copy-start.8) | copy-done | bytes 1048
  5.0 0.5 %slice.3 = s32[1]{0:T(128)} slice(s32[256]{0:T(256)S(1)} %copy-done.8), slice={[0:1]} | slice | bytes 8 | tf_op jit(solution)/shard_map/slice | solution.py:450
  6.2 6.2 %conditional.1 = (f32[72,256]{1,0:T(8,128)}) conditional(s32[]{:T(128)} %clamp.3, f32[72,256]{1,0:T(8,128)S(1)} %get-tuple-element.45, f32[72,256]{1,0:T(8,128)S(1)} %get-tuple-element.45, f32[72,256]{1,0:T(8,128)S(1)} %get-tuple-element.45, f32[72,256]{1,0:T(8,128)S(1)} %get-tuple-element.45, ...), branch_computations={%region_0.1_spmd, %region_1.2_spmd, %region_2.3_spmd, %region_3.4_... | conditional | bytes 294960 | solution.py:470
  6.2 3.0 %collective-permute-start.4 = (f32[72,256]{1,0:T(8,128)S(1)}, f32[72,256]{1,0:T(8,128)}, u32[]{:S(2)}, u32[]{:S(2)}) collective-permute-start(f32[72,256]{1,0:T(8,128)S(1)} %param.4), channel_id=1, source_target_pairs={{1,2},{2,1},{3,4},{4,3},{5,6},{6,5},{7,31},{9,10},{10,9},{11,12},{... | collective-permute-start | bytes 221192 | tf_op jit(solution)/shard_map/cond/branch_4_fun/ppermute | solution.py:444
  9.2 3.2 %collective-permute-done.4 = f32[72,256]{1,0:T(8,128)} collective-permute-done((f32[72,256]{1,0:T(8,128)S(1)}, f32[72,256]{1,0:T(8,128)}, u32[]{:S(2)}, u32[]{:S(2)}) %collective-permute-start.4) | collective-permute-done | bytes 73760 | tf_op jit(solution)/shard_map/cond/branch_4_fun/ppermute | solution.py:444
  12.4 0.0 collective-permute-done.16.a_ref
  12.4 0.0 copy-done
  12.4 0.0 copy-start.5
  12.5 1.1 %copy-done.5 = f32[10,64,256]{2,1,0:T(8,128)S(1)} copy-done((f32[10,64,256]{2,1,0:T(8,128)S(1)}, f32[10,64,256]{2,1,0:T(8,128)}, u32[]{:S(2)}) %copy-start.5) | copy-done | bytes 655384
  13.5 6.8 %advect.1 = (f32[10,64,256]{2,1,0:T(8,128)S(1)}, f32[10,64,256]{2,1,0:T(8,128)S(1)}, f32[32,256]{1,0:T(8,128)S(1)}, f32[72,128]{1,0:T(8,128)S(1)}, f32[72,128]{1,0:T(8,128)S(1)}) custom-call(s32[1]{0:T(128)S(6)} %copy.30.hinge_ref, f32[10,64,256]{2,1,0:T(8,128)S(1)} %copy-done.4, f32[10,64,256]{2,1,0:T(8,128)S(1)} %copy-done.5, f32[10,64,256]{2,1,0:T(8,128)S(1)} %copy-done, ...), custom_call_target="tpu_custom_call" | custom-call | tf_op jit(solution)/shard_map/advect/pallas_call | solution.py:473
  20.3 0.3 collective-permute-start.17
  20.6 8.3 %collective-permute-start.18 = (f32[72,128]{1,0:T(8,128)S(1)}, f32[72,128]{1,0:T(8,128)S(1)}, u32[]{:S(2)}, u32[]{:S(2)}) collective-permute-start(f32[72,128]{1,0:T(8,128)S(1)} %get-tuple-element.50.d_own_ref), channel_id=1, source_target_pairs={{0,120},{8,16},{16,8},{24,32},{32,24},{40,48},{48,40},{56,64},{64,... | collective-permute-start | bytes 110600 | tf_op jit(solution)/shard_map/ppermute | solution.py:434
  29.0 0.0 collective-permute-done.17.c_ref
  29.0 1.6 %collective-permute-done.18.d_ref = f32[72,128]{1,0:T(8,128)S(1)} collective-permute-done((f32[72,128]{1,0:T(8,128)S(1)}, f32[72,128]{1,0:T(8,128)S(1)}, u32[]{:S(2)}, u32[]{:S(2)}) %collective-permute-start.18) | collective-permute-done | bytes 36896 | tf_op jit(solution)/shard_map/ppermute | solution.py:434
  30.6 0.7 %copy-done.6 = f32[10]{0:T(128)S(1)} copy-done((f32[10]{0:T(128)S(1)}, f32[10]{0:T(128)}, u32[]{:S(2)}) %copy-start.6) | copy-done | bytes 64
  31.3 0.0 copy-done.7
  31.3 6.8 %finish.1 = (f32[10,64,256]{2,1,0:T(8,128)}, f32[10,64,256]{2,1,0:T(8,128)}, f32[10,64,256]{2,1,0:T(8,128)}, f32[10,64,256]{2,1,0:T(8,128)}) custom-call(f32[10]{0:T(128)S(1)} %copy-done.6, f32[1,64]{1,0:T(1,128)S(1)} %bitcast.2, f32[10,64,256]{2,1,0:T(8,128)S(1)} %get-tuple-element.46.heat_ref, f32[10,64,256]{2,1,0:T(8,128)S(1)} %get-tuple-element.47.salt_ref, ...), custom_call_target="tpu_custom_call" | custom-call | tf_op jit(solution)/shard_map/finish/pallas_call | solution.py:496
  (7 shorter events, 0.0 us)
Async XLA Ops:
  1.3 11.1 %copy-start = (f32[10,64,256]{2,1,0:T(8,128)S(1)}, f32[10,64,256]{2,1,0:T(8,128)}, u32[]{:S(2)}) copy-start(f32[10,64,256]{2,1,0:T(8,128)} %east_ref.3) | copy-start | bytes 1966084
  1.3 11.1 %copy-start.1 = (f32[10,64,256]{2,1,0:T(8,128)S(1)}, f32[10,64,256]{2,1,0:T(8,128)}, u32[]{:S(2)}) copy-start(f32[10,64,256]{2,1,0:T(8,128)} %north_ref.3) | copy-start | bytes 1966084
  1.3 11.1 %copy-start.2 = (s32[10,64,256]{2,1,0:T(8,128)S(1)}, s32[10,64,256]{2,1,0:T(8,128)}, u32[]{:S(2)}) copy-start(s32[10,64,256]{2,1,0:T(8,128)} %wet_ref.3) | copy-start | bytes 1966084
  1.3 11.1 %copy-start.3 = (f32[9,64,256]{2,1,0:T(8,128)S(1)}, f32[9,64,256]{2,1,0:T(8,128)}, u32[]{:S(2)}) copy-start(f32[9,64,256]{2,1,0:T(8,128)} %mix_ref.3) | copy-start | bytes 1769476
  1.3 11.1 %copy-start.4 = (f32[10,64,256]{2,1,0:T(8,128)S(1)}, f32[10,64,256]{2,1,0:T(8,128)}, u32[]{:S(2)}) copy-start(f32[10,64,256]{2,1,0:T(8,128)} %heat_ref.1) | copy-start | bytes 1966084
  3.9 8.5 %collective-permute-start.16 = (f32[72,256]{1,0:T(8,128)}, f32[72,256]{1,0:T(8,128)S(1)}, u32[]{:S(2)}, u32[]{:S(2)}) collective-permute-start(f32[72,256]{1,0:T(8,128)} %get-tuple-element.44), channel_id=1, source_target_pairs={{0,1},{1,0},{2,3},{3,2},{4,5},{5,4},{6,7},{7,6},{8,9},{9,8},{10,11... | collective-permute-start | bytes 221192 | tf_op jit(solution)/shard_map/ppermute | solution.py:434
  4.3 0.7 %copy-start.8 = (s32[256]{0:T(256)S(1)}, s32[256]{0:T(256)}, u32[]{:S(2)}) copy-start(s32[256]{0:T(256)} %param.35) | copy-start | bytes 3076
  6.2 6.2 %collective-permute-start.4 = (f32[72,256]{1,0:T(8,128)S(1)}, f32[72,256]{1,0:T(8,128)}, u32[]{:S(2)}, u32[]{:S(2)}) collective-permute-start(f32[72,256]{1,0:T(8,128)S(1)} %param.4), channel_id=1, source_target_pairs={{1,2},{2,1},{3,4},{4,3},{5,6},{6,5},{7,31},{9,10},{10,9},{11,12},{... | collective-permute-start | bytes 221192 | tf_op jit(solution)/shard_map/cond/branch_4_fun/ppermute | solution.py:444
  12.4 1.1 %copy-start.5 = (f32[10,64,256]{2,1,0:T(8,128)S(1)}, f32[10,64,256]{2,1,0:T(8,128)}, u32[]{:S(2)}) copy-start(f32[10,64,256]{2,1,0:T(8,128)} %salt_ref.1) | copy-start | bytes 1966084
  20.3 8.6 %collective-permute-start.17 = (f32[72,128]{1,0:T(8,128)S(1)}, f32[72,128]{1,0:T(8,128)S(1)}, u32[]{:S(2)}, u32[]{:S(2)}) collective-permute-start(f32[72,128]{1,0:T(8,128)S(1)} %get-tuple-element.49.c_own_ref), channel_id=1, source_target_pairs={{0,8},{8,0},{16,24},{24,16},{32,40},{40,32},{48,56},{56,48},{64,72... | collective-permute-start | bytes 110600 | tf_op jit(solution)/shard_map/ppermute | solution.py:434
  20.6 10.0 %collective-permute-start.18 = (f32[72,128]{1,0:T(8,128)S(1)}, f32[72,128]{1,0:T(8,128)S(1)}, u32[]{:S(2)}, u32[]{:S(2)}) collective-permute-start(f32[72,128]{1,0:T(8,128)S(1)} %get-tuple-element.50.d_own_ref), channel_id=1, source_target_pairs={{0,120},{8,16},{16,8},{24,32},{32,24},{40,48},{48,40},{56,64},{64,... | collective-permute-start | bytes 110600 | tf_op jit(solution)/shard_map/ppermute | solution.py:434
  30.6 0.7 %copy-start.6 = (f32[10]{0:T(128)S(1)}, f32[10]{0:T(128)}, u32[]{:S(2)}) copy-start(f32[10]{0:T(128)} %thick_ref.1) | copy-start | bytes 124
  30.6 0.7 %copy-start.7 = (f32[64]{0:T(128)S(1)}, f32[64]{0:T(128)}, u32[]{:S(2)}) copy-start(f32[64]{0:T(128)} %param.33) | copy-start | bytes 772
